TPU v7x, 128 devices: a whole 4x4x4 slice. The times are simulated.
128 devices in a mesh: fsdp: 16 (over z_hi, y, core), seq: 8 (over z_lo, x).
Axes of the slice: x: 4, y: 4, z: 4 (z_hi: 2, z_lo: 2; z = z_hi * 2 + z_lo), core: 2. Of those that a mesh axis runs over, the one named last changes fastest.
Arguments:
- tokens: bfloat16 [2048, 8192], P('seq', 'fsdp'), may hold values from -6 to 6
- lang_ids: int32 [2048], P('seq'), may hold values from 0 to 1
- norm_gain: float32 [8192], replicated, may hold values from 0.1 to 1.9
- gate_weight: bfloat16 [8192, 12288], P('seq', 'fsdp'), may hold values from -0.0625 to 0.0625
- up_weight: bfloat16 [8192, 12288], P('seq', 'fsdp'), may hold values from -0.0625 to 0.0625
Outputs:
- gram_in: float32 [8192, 8192], P('fsdp', 'seq')
- gram_hidden: float32 [12288, 12288], P('fsdp', 'seq')
All inputs are finite; a program needn't handle non-finite values.
Results may differ from a plain program's by a relative error of at most 0.0068.
Values may be sent and summed in bfloat16 or wider, within the bound.
A program may use at most 128 MiB of HBM per device.

v0:
```python
import jax
import jax.numpy as jnp
from jax import lax
from jax.sharding import PartitionSpec as P


def spread(shard, axis, root):
    mine = lax.axis_index(axis) == root
    return lax.psum(jnp.where(mine, shard, jnp.zeros_like(shard)), axis)


def tile_gram(left, parts, total):
    right = jnp.concatenate(parts, axis=1)
    return jnp.einsum("ti,tj->ij", left, right, preferred_element_type=jnp.float32) / total


def per_device(tokens, lang_ids, norm_gain, gate_weight, up_weight):
    rows = lax.all_gather(tokens, "fsdp", axis=1, tiled=True)
    values = rows.astype(jnp.float32)
    scale = lax.rsqrt(jnp.mean(values * values, axis=1, keepdims=True) + 1e-05)
    normed = (values * scale * norm_gain[None, :]).astype(jnp.bfloat16)
    keep = (lang_ids == 0).astype(jnp.bfloat16)[:, None]
    n_fsdp = lax.axis_size("fsdp")
    n_seq = lax.axis_size("seq")
    fsdp_place = lax.axis_index("fsdp")
    seq_place = lax.axis_index("seq")
    feat_width = normed.shape[1] // n_fsdp
    own_in = lax.dynamic_slice_in_dim(normed, fsdp_place * feat_width, feat_width, 1) * keep
    gate = jnp.dot(
        normed,
        lax.all_gather(gate_weight, "seq", axis=0, tiled=True),
        preferred_element_type=jnp.float32,
    )
    up = jnp.dot(
        normed,
        lax.all_gather(up_weight, "seq", axis=0, tiled=True),
        preferred_element_type=jnp.float32,
    )
    hidden = (jax.nn.silu(gate) * up).astype(jnp.bfloat16)
    own_hidden = hidden * keep
    repeat = n_fsdp // n_seq
    in_all = lax.all_gather(own_in, "seq", axis=0, tiled=True)
    in_parts = [spread(in_all, "fsdp", seq_place * repeat + offset) for offset in range(repeat)]
    total = float(in_all.shape[0])
    gram_in = tile_gram(in_all, in_parts, total)
    hid_all = lax.all_gather(own_hidden, "seq", axis=0, tiled=True)
    hid_parts = [spread(hid_all, "fsdp", seq_place * repeat + offset) for offset in range(repeat)]
    gram_hidden = tile_gram(hid_all, hid_parts, total)
    return (gram_in, gram_hidden)


def solution(mesh):
    in_specs = (P("seq", "fsdp"), P("seq"), P(), P("seq", "fsdp"), P("seq", "fsdp"))
    out_specs = (P("fsdp", "seq"), P("fsdp", "seq"))
    return jax.shard_map(
        per_device, mesh=mesh, in_specs=in_specs, out_specs=out_specs, check_vma=False
    )
```

profile of v0, /device:TPU:1, one launch (start us, length us, event | category | flops | bytes accessed | tf_op | source)
XLA Modules:
  0.0 617.6 jit_solution(5000312425539968266)
XLA Ops:
  7.2 0.0 copy-start.4
  7.2 0.0 all-gather.6.cloned.1.call-start
  7.2 0.7 all-gather.6.cloned.1.call-update
  7.9 0.0 all-gather.10.cloned.1.call-start
  8.0 0.7 all-gather.10.cloned.1.call-update
  8.7 0.0 all-gather.12.cloned.1.call-start
  8.7 0.7 all-gather.12.cloned.1.call-update
  9.4 0.0 all-gather.8.cloned.1.call-start
  9.4 0.7 compare_convert_fusion
  10.1 63.0 %all-gather.6.cloned.1.call-done = bf16[256,8192]{1,0:T(8,128)(2,1)} async-done(((bf16[256,512]{1,0:T(8,128)(2,1)}), bf16[256,8192]{1,0:T(8,128)(2,1)}) %all-gather.6.cloned.1.call-update) | async-done | bytes 4194320 | tf_op jit(solution)/shard_map/all_gather | solution.py:18
  73.2 0.0 copy-start
  73.2 3.3 fusion
  76.4 0.0 copy-done.4
  76.4 0.2 copy-done
  76.6 1.2 fusion.2
  77.8 0.0 copy-start.1
  77.8 2.0 copy-done.1
  79.8 0.8 dynamic-slice_multiply_fusion
  80.6 0.0 all-gather.8.cloned.1.call-update
  80.7 0.0 all-gather.14.cloned.1.call-start
  80.7 123.4 %all-gather.10.cloned.1.call-done = bf16[8192,768]{1,0:T(8,128)(2,1)} async-done(((bf16[1024,768]{1,0:T(8,128)(2,1)}), bf16[8192,768]{1,0:T(8,128)(2,1)}) %all-gather.10.cloned.1.call-update) | async-done | bytes 12582928 | tf_op jit(solution)/shard_map/all_gather | solution.py:31
  204.1 8.8 %fusion.21 = f32[256,768]{1,0:T(8,128)S(1)} fusion(bf16[256,8192]{1,0:T(8,128)(2,1)} %copy-done.1, bf16[8192,768]{1,0:T(8,128)(2,1)} %all-gather.10.cloned.1.call-done), kind=kOutput, calls=%fused_computation.27 | convolution fusion | flops 3221225472 | bytes 17563648 | tf_op jit(solution)/shard_map/dot_general | solution.py:29
  212.9 122.8 %all-gather.12.cloned.1.call-done = bf16[8192,768]{1,0:T(8,128)(2,1)} async-done(((bf16[1024,768]{1,0:T(8,128)(2,1)}), bf16[8192,768]{1,0:T(8,128)(2,1)}) %all-gather.12.cloned.1.call-update) | async-done | bytes 12582928 | tf_op jit(solution)/shard_map/all_gather | solution.py:36
  335.8 10.1 %fusion.18 = bf16[256,768]{1,0:T(8,128)(2,1)} fusion(bf16[256,8192]{1,0:T(8,128)(2,1)} %copy-done.1, bf16[8192,768]{1,0:T(8,128)(2,1)} %all-gather.12.cloned.1.call-done, f32[256,768]{1,0:T(8,128)S(1)} %fusion.21, bf16[256]{0:T(256)(128)(2,1)S(1)} %compare_convert_fusion), kind=kOutput, calls=%fused_computation.21 | convolution fusion | flops 3222601728 | bytes 17957376 | tf_op jit(solution)/shard_map/dot_general | solution.py:34
  345.9 0.0 all-gather.14.cloned.1.call-update
  345.9 0.0 all-reduce.3.cloned.1.call-start
  346.0 27.4 %all-gather.8.cloned.1.call-done = bf16[2048,512]{1,0:T(8,128)(2,1)} async-done(((bf16[256,512]{1,0:T(8,128)(2,1)}), bf16[2048,512]{1,0:T(8,128)(2,1)}) %all-gather.8.cloned.1.call-update) | async-done | bytes 2097168 | tf_op jit(solution)/shard_map/all_gather | solution.py:42
  373.4 3.9 broadcast_select_fusion.3
  377.2 43.4 %all-gather.14.cloned.1.call-done = bf16[2048,768]{1,0:T(8,128)(2,1)} async-done(((bf16[256,768]{1,0:T(8,128)(2,1)}), bf16[2048,768]{1,0:T(8,128)(2,1)}) %all-gather.14.cloned.1.call-update) | async-done | bytes 3145744 | tf_op jit(solution)/shard_map/all_gather | solution.py:46
  420.6 5.0 broadcast_select_fusion.1
  425.6 0.0 copy-start.2
  425.6 0.0 all-reduce.3.cloned.1.call-update
  425.6 171.7 %all-reduce.3.cloned.1.call-done = (bf16[2048,512]{1,0:T(8,128)(2,1)}, bf16[2048,512]{1,0:T(8,128)(2,1)}, bf16[2048,768]{1,0:T(8,128)(2,1)}, bf16[2048,768]{1,0:T(8,128)(2,1)}) async-done(((bf16[2048,512]{1,0:T(8,128)(2,1)}, bf16[2048,512]{1,0:T(8,128)(2,1)}, bf16[2048,768]{1,0:T(8,128)(2,1)}, bf16[2048,768]{1,0:T(8,128)(2,1)}), (bf16[2048,512]{1,0:T(8,128)(2,1)}, bf16[2048,512]{1,0:T(8,128)(2,1)}, ...) | async-done | bytes 10485776 | tf_op jit(solution)/shard_map/psum | solution.py:9
  597.3 0.0 copy-done.2
  597.3 0.0 copy-start.3
  597.3 0.0 copy-start.5
  597.3 0.0 copy-start.6
  597.3 9.7 %fusion.11 = f32[768,1536]{1,0:T(8,128)} fusion(bf16[2048,768]{1,0:T(8,128)(2,1)S(1)} %copy-done.2, bf16[2048,768]{1,0:T(8,128)(2,1)} %get-tuple-element.4, bf16[2048,768]{1,0:T(8,128)(2,1)} %get-tuple-element.5), kind=kOutput, calls=%fused_computation.13 | convolution fusion | flops 4845600768 | bytes 14155776 | tf_op jit(solution)/shard_map/ti,tj->ij/dot_general | solution.py:14
  607.1 0.0 copy-done.3
  607.1 0.0 copy-done.5
  607.1 0.0 copy-done.6
  607.1 3.7 fusion.14
  (1 shorter events, 0.0 us)
Async XLA Ops:
  7.2 69.3 %copy-start.4 = (f32[8192]{0:T(1024)S(1)}, f32[8192]{0:T(1024)}, u32[]{:S(2)}) copy-start(f32[8192]{0:T(1024)} %param.7) | copy-start | bytes 98308
  7.2 66.0 %all-gather.6.cloned.1.call-start = ((), (), s32[]{:S(2)}) async-start(), calls=%async_computation | async-start | bytes 4456448 | tf_op jit(solution)/shard_map/all_gather | solution.py:18
  7.9 196.2 %all-gather.10.cloned.1.call-start = ((), (), s32[]{:S(2)}) async-start(), calls=%async_computation.2 | async-start | bytes 14155776 | tf_op jit(solution)/shard_map/all_gather | solution.py:31
  8.7 327.1 %all-gather.12.cloned.1.call-start = ((), (), s32[]{:S(2)}) async-start(), calls=%async_computation.3 | async-start | bytes 14155776 | tf_op jit(solution)/shard_map/all_gather | solution.py:36
  9.4 364.0 %all-gather.8.cloned.1.call-start = ((), (), s32[]{:S(2)}) async-start(), calls=%async_computation.1 | async-start | bytes 2359296 | tf_op jit(solution)/shard_map/all_gather | solution.py:42
  73.2 3.4 copy-start
  77.8 2.0 copy-start.1
  80.7 339.9 %all-gather.14.cloned.1.call-start = ((), (), s32[]{:S(2)}) async-start(), calls=%async_computation.4 | async-start | bytes 3538944 | tf_op jit(solution)/shard_map/all_gather | solution.py:46
  345.9 251.4 %all-reduce.3.cloned.1.call-start = ((), (), s32[]{:S(2)}) async-start(), calls=%async_computation.5 | async-start | bytes 20971520 | tf_op jit(solution)/shard_map/psum | solution.py:9
  425.6 171.7 %copy-start.2 = (bf16[2048,768]{1,0:T(8,128)(2,1)S(1)}, bf16[2048,768]{1,0:T(8,128)(2,1)}, u32[]{:S(2)}) copy-start(bf16[2048,768]{1,0:T(8,128)(2,1)} %all-gather.14.cloned.1.call-done) | copy-start | bytes 9437188
  597.3 9.7 %copy-start.3 = (bf16[2048,512]{1,0:T(8,128)(2,1)S(1)}, bf16[2048,512]{1,0:T(8,128)(2,1)}, u32[]{:S(2)}) copy-start(bf16[2048,512]{1,0:T(8,128)(2,1)} %all-gather.8.cloned.1.call-done) | copy-start | bytes 6291460
  597.3 9.7 %copy-start.5 = (bf16[2048,512]{1,0:T(8,128)(2,1)S(1)}, bf16[2048,512]{1,0:T(8,128)(2,1)}, u32[]{:S(2)}) copy-start(bf16[2048,512]{1,0:T(8,128)(2,1)} %get-tuple-element.2) | copy-start | bytes 6291460
  597.3 9.7 %copy-start.6 = (bf16[2048,512]{1,0:T(8,128)(2,1)S(1)}, bf16[2048,512]{1,0:T(8,128)(2,1)}, u32[]{:S(2)}) copy-start(bf16[2048,512]{1,0:T(8,128)(2,1)} %get-tuple-element.3) | copy-start | bytes 6291460
Sparse Core Ops, SparseCore 0:
  10.3 62.8 all-gather.5
  74.8 129.2 all-gather.9
  205.8 129.9 all-gather.11
  337.9 35.4 all-gather.7
  374.8 45.6 all-gather.13
  425.7 171.5 all-reduce.2
where the time goes:
time: 619 us; the launch traced here: 618 us
  waiting for transfers between devices  554 us (89%)
  matrix products  32.3 us (5%)
  other arithmetic  14.8 us (2%)
  between operations  14.2 us (2%)
    psum x1, waiting for transfers between devices, spread(): return lax.psum(jnp.where(mine, shard, jnp.zeros_like(shard)), axis)  172 us
    all_gather x1, waiting for transfers between devices, per_device(): lax.all_gather(gate_weight, 'seq', axis=0, tiled=True)  123 us
    all_gather x1, waiting for transfers between devices, per_device(): lax.all_gather(up_weight, 'seq', axis=0, tiled=True)  123 us
    all_gather x1, waiting for transfers between devices, per_device(): rows = lax.all_gather(tokens, 'fsdp', axis=1, tiled=True)  63 us
    all_gather x1, waiting for transfers between devices, per_device(): hid_all = lax.all_gather(own_hidden, 'seq', axis=0, tiled=True)  43.4 us
    all_gather x1, waiting for transfers between devices, per_device(): in_all = lax.all_gather(own_in, 'seq', axis=0, tiled=True)  27.4 us
    dot_general x2, matrix products, tile_gram(): jnp.einsum('ti,tj->ij', left, right, preferred_element_type=jnp.float32)  13.4 us
  transfers between devices with their start and end apart: 6, of which 6 were waited for; matrix products, arithmetic and copies ran while one was open for 5% of the time, Pallas kernels for 0%

commit v1 on v0

v1 whole, which is shorter than its diff:
```python
import functools

import jax
import jax.numpy as jnp
from jax import lax
from jax.experimental import pallas as pl
from jax.experimental.pallas import tpu as pltpu
from jax.sharding import PartitionSpec as P

MESH = pl.DeviceIdType.MESH
F32 = jnp.float32
BF16 = jnp.bfloat16
TOK = 256
FEAT = 512
COLS = 768
WA, WB = 512, 256
DEPTH = 1024
TOTAL = 2048
D = 8192

_RANGES = {}
_next = 0
for _name, _count in (
    ("z", 3), ("ss", 8), ("rsa", 4), ("rsb", 4), ("rsa2", 4), ("rsb2", 1),
    ("Xcy", 4), ("Xrx", 4), ("Xax", 4), ("Xsib", 4), ("Xrz", 4),
    ("Az", 3), ("Acy", 4), ("Arx", 4), ("Aax", 4), ("Asib", 4), ("Arz", 4),
    ("Bz", 3), ("Bcy", 4), ("Brx", 4), ("Bax", 4), ("Bsib", 4), ("Brz", 4),
):
    _RANGES[_name] = _next
    _next += _count
N_SEM = _next


def mod4(v):
    return lax.rem(v + 8, 4)


def kernel(
    tok_ref, gain_ref, wg_hbm, wu_hbm,
    xf_out, xs_out, hf_out, hs_out,
    raw, nb, ss, xc, xf, xs, wg, wu, pa, pb, ra, ra2, rb, rb2, sbf,
    hba, hca, hfa, hsa, hbb, hcb, hfb, hsb,
    ssem, rsem, wsem, osem,
):
    f = lax.axis_index("fsdp")
    s = lax.axis_index("seq")
    zh, y, c = f // 8, lax.rem(f // 2, 4), lax.rem(f, 2)
    zl, x = s // 4, lax.rem(s, 4)

    def dev(zh_, y_, c_, zl_, x_):
        return (zh_ * 8 + y_ * 2 + c_, zl_ * 4 + x_)

    z_src = [(zh, 1 - zl), (1 - zh, zl), (1 - zh, 1 - zl)]
    z_peers = [dev(a, y, c, b, x) for a, b in z_src]
    partner = z_peers[0]
    sib = dev(zh, y, 1 - c, zl, x)

    def x_peer(d):
        return dev(zh, y, c, zl, mod4(x + d))

    def y_peer(d, e=0):
        return dev(zh, mod4(y + d), c if e == 0 else 1 - c, zl, x)

    pending = []

    def remote(src, dst, name, i, device):
        base = _RANGES[name]
        return pltpu.make_async_remote_copy(
            src_ref=src, dst_ref=dst, send_sem=ssem.at[base + i], recv_sem=rsem.at[base + i],
            device_id=device, device_id_type=MESH,
        )

    def send(src, dst, name, i, device):
        copy = remote(src, dst, name, i, device)
        copy.start()
        pending.append(copy)

    def arrived(dst, name, i):
        remote(dst, dst, name, i, sib).wait_recv()

    w_copies = [
        pltpu.make_async_copy(wg_hbm, wg, wsem.at[0]),
        pltpu.make_async_copy(wu_hbm, wu, wsem.at[1]),
    ]
    for copy in w_copies:
        copy.start()

    barrier = pltpu.get_barrier_semaphore()
    peers = list(z_peers) + [x_peer(d) for d in (1, 2, 3)]
    peers += [y_peer(d, e) for d in range(4) for e in range(2) if (d, e) != (0, 0)]
    for peer in peers:
        pl.semaphore_signal(barrier, inc=1, device_id=peer, device_id_type=MESH)
    raw[zh, zl] = tok_ref[...]
    pl.semaphore_wait(barrier, len(peers))

    for i, peer in enumerate(z_peers):
        send(raw.at[zh, zl], raw.at[zh, zl], "z", i, peer)
    for i, (a, b) in enumerate(z_src):
        arrived(raw.at[a, b], "z", i)

    slot = y * 2 + c
    for t in range(2):
        v0 = raw[0, t].astype(F32)
        v1 = raw[1, t].astype(F32)
        sq = v0 * v0 + v1 * v1
        sq = sq[:, 0:128] + sq[:, 128:256] + sq[:, 256:384] + sq[:, 384:512]
        row = jnp.sum(jnp.transpose(sq), axis=0, keepdims=True)
        ss[slot, :, t * TOK:(t + 1) * TOK] = jnp.broadcast_to(row, (8, TOK))
    for d in range(4):
        for e in range(2):
            if (d, e) != (0, 0):
                send(ss.at[slot], ss.at[slot], "ss", d * 2 + e, y_peer(d, e))
    for d in range(4):
        for e in range(2):
            if (d, e) != (0, 0):
                arrived(ss.at[mod4(y - d) * 2 + (c if e == 0 else 1 - c)], "ss", d * 2 + e)
    total = ss[0]
    for i in range(1, 8):
        total = total + ss[i]
    scale = lax.rsqrt(total / float(D) + 1e-05)
    for t in range(2):
        col = jnp.transpose(jnp.broadcast_to(scale[0:1, t * TOK:(t + 1) * TOK], (128, TOK)))
        for b in range(2):
            g = gain_ref[b * 8 + y * 2 + c]
            for k in range(FEAT // 128):
                lanes = slice(k * 128, (k + 1) * 128)
                v = raw[b, t, :, lanes].astype(F32)
                nb[b, t, :, lanes] = (v * col * g[:, lanes]).astype(BF16)

    def row_first(q, own, row):
        for d in (1, 3, 2):
            send(own.at[zh, zl], row.at[x, zl], q + "rx", d, x_peer(d))

    def column_first(q, own, col):
        for d in (1, 3, 2):
            send(own.at[zl], col.at[y], q + "cy", d, y_peer(d))
        col[y] = own[zl]

    def column_wait(q, col, yy):
        d = mod4(y - yy)

        @pl.when(d != 0)
        def _():
            arrived(col.at[yy], q + "cy", d)

    def column_second(q, col, panel):
        for d in (1, 3, 2):
            to = mod4(x + d)
            column_wait(q, col, to)
            send(col.at[to], panel.at[c, x], q + "ax", d, x_peer(d))
        column_wait(q, col, x)
        send(col.at[x], panel.at[c, x], q + "sib", 0, sib)
        panel[c, x] = col[x]

    def column_third(q, panel, d):
        at = mod4(x - d)
        arrived(panel.at[c, at], q + "ax", d)
        send(panel.at[c, at], panel.at[c, at], q + "sib", d, sib)

    def column_done(q, panel, d):
        arrived(panel.at[1 - c, mod4(x - d)], q + "sib", d)

    def row_second(q, own, row):
        row[x] = own[zh]
        for d in (1, 3, 2):
            at = mod4(x - d)
            arrived(row.at[at, zl], q + "rx", d)
            send(row.at[at, zl], row.at[at, zl], q + "rz", d, partner)

    def row_done(q, row):
        for d in (1, 3, 2):
            arrived(row.at[mod4(x - d), 1 - zl], q + "rz", d)

    column_first("X", nb, xc)
    row_first("X", nb, xf)
    column_second("X", xc, xs)
    row_second("X", nb, xf)
    for copy in w_copies:
        copy.wait()

    for d in (0, 1, 3, 2):
        if d:
            column_third("X", xs, d)
        column_done("X", xs, d)
        at = mod4(x - d)

        def half(t, _):
            a0 = xs[0, at, t]
            a1 = xs[1, at, t]

            def product(w, n):
                lanes = slice(n * 256, (n + 1) * 256)
                return (
                    jnp.dot(a0, w[0:FEAT, lanes], preferred_element_type=F32)
                    + jnp.dot(a1, w[FEAT:DEPTH, lanes], preferred_element_type=F32)
                ).astype(BF16)

            for n in range(2):
                pa[at, t, :, n * 256:(n + 1) * 256] = product(wg, n)
                pa[at, t, :, WA + n * 256:WA + (n + 1) * 256] = product(wu, n)
            pb[at, t, :, 0:WB] = product(wg, 2)
            pb[at, t, :, WB:2 * WB] = product(wu, 2)
            return 0

        lax.fori_loop(0, 2, half, 0)
        send(pa.at[at, 1 - zl], ra.at[at], "rsa", d, partner)
        if d:
            send(pb.at[at], rb.at[x], "rsb", 4 - d, dev(zh, y, c, zl, at))

    row_done("X", xf)
    outs = []

    def store(src, dst):
        copy = pltpu.make_async_copy(src, dst, osem.at[len(outs)])
        copy.start()
        outs.append(copy)

    store(xf, xf_out)
    for cc in range(2):
        store(xs.at[cc], xs_out.at[:, :, :, pl.ds(cc * FEAT, FEAT)])

    def second(d):
        at = mod4(x - d)
        arrived(ra.at[at], "rsa", d)
        if d:
            pa[at, zl] = (pa[at, zl].astype(F32) + ra[at].astype(F32)).astype(BF16)
            send(pa.at[at, zl], ra2.at[x], "rsa2", 4 - d, dev(zh, y, c, zl, at))

    def swiglu(v, w):
        g, u = v[:, 0:w], v[:, w:2 * w]
        return (g / (1.0 + jnp.exp(-g)) * u).astype(BF16)

    second(0)
    second(1)
    for d in (1, 3, 2):
        arrived(rb.at[mod4(x - d)], "rsb", d)

    def sum_b(t):
        v = pb[x, t].astype(F32)
        for d in (1, 2, 3):
            v = v + rb[mod4(x - d), t].astype(F32)
        return v

    sbf[...] = sum_b(1 - zl).astype(BF16)
    send(sbf, rb2, "rsb2", 0, partner)
    second(3)
    second(2)
    arrived(rb2, "rsb2", 0)
    hbb[zh, zl] = swiglu(sum_b(zl) + rb2[...].astype(F32), WB)

    def z_send(q, own):
        for i, peer in enumerate(z_peers):
            send(own.at[zh, zl], own.at[zh, zl], q + "z", i, peer)

    def z_wait(q, own):
        for i, (a, b) in enumerate(z_src):
            arrived(own.at[a, b], q + "z", i)

    z_send("B", hbb)
    row_first("B", hbb, hfb)

    for d in (1, 3, 2):
        arrived(ra2.at[mod4(x - d)], "rsa2", d)
    va = pa[x, zl].astype(F32) + ra[x].astype(F32)
    for d in (1, 2, 3):
        va = va + ra2[mod4(x - d)].astype(F32)
    hba[zh, zl] = swiglu(va, WA)
    z_send("A", hba)
    row_first("A", hba, hfa)

    z_wait("B", hbb)
    column_first("B", hbb, hcb)
    z_wait("A", hba)
    column_first("A", hba, hca)
    column_second("B", hcb, hsb)
    row_second("B", hbb, hfb)
    column_second("A", hca, hsa)
    row_second("A", hba, hfa)
    for d in (1, 3, 2):
        column_third("B", hsb, d)
    for d in (0, 1, 3, 2):
        column_done("B", hsb, d)
    row_done("B", hfb)
    store(hfb, hf_out.at[:, :, :, pl.ds(WA, WB)])
    for cc in range(2):
        store(hsb.at[cc], hs_out.at[:, :, :, pl.ds(cc * COLS + WA, WB)])
    for d in (1, 3, 2):
        column_third("A", hsa, d)
    for d in (0, 1, 3, 2):
        column_done("A", hsa, d)
    row_done("A", hfa)
    store(hfa, hf_out.at[:, :, :, pl.ds(0, WA)])
    for cc in range(2):
        store(hsa.at[cc], hs_out.at[:, :, :, pl.ds(cc * COLS, WA)])
    for copy in pending:
        copy.wait_send()
    for copy in outs:
        copy.wait()


def panels(tokens, gain, gate_weight, up_weight):
    def vm(*shape, dtype=BF16):
        return pltpu.VMEM(shape, dtype)

    shapes = [(4, 2, TOK, FEAT), (4, 2, TOK, 2 * FEAT), (4, 2, TOK, COLS), (4, 2, TOK, 2 * COLS)]
    any_spec = pl.BlockSpec(memory_space=pl.ANY)
    vmem_spec = pl.BlockSpec(memory_space=pltpu.VMEM)
    scratch = [
        vm(2, 2, TOK, FEAT), vm(2, 2, TOK, FEAT), vm(8, 8, 2 * TOK, dtype=F32),
        vm(4, 2, TOK, FEAT), vm(4, 2, TOK, FEAT), vm(2, 4, 2, TOK, FEAT),
        vm(DEPTH, COLS), vm(DEPTH, COLS),
        vm(4, 2, TOK, 2 * WA), vm(4, 2, TOK, 2 * WB), vm(4, TOK, 2 * WA), vm(4, TOK, 2 * WA),
        vm(4, 2, TOK, 2 * WB), vm(TOK, 2 * WB), vm(TOK, 2 * WB),
    ]
    for w in (WA, WB):
        scratch += [vm(2, 2, TOK, w), vm(4, 2, TOK, w), vm(4, 2, TOK, w), vm(2, 4, 2, TOK, w)]
    scratch += [
        pltpu.SemaphoreType.DMA((N_SEM,)), pltpu.SemaphoreType.DMA((N_SEM,)),
        pltpu.SemaphoreType.DMA((2,)), pltpu.SemaphoreType.DMA((9,)),
    ]
    return pl.pallas_call(
        kernel,
        out_shape=[jax.ShapeDtypeStruct(shape, BF16) for shape in shapes],
        in_specs=[vmem_spec, vmem_spec, any_spec, any_spec],
        out_specs=[any_spec] * 4,
        scratch_shapes=scratch,
        compiler_params=pltpu.CompilerParams(
            collective_id=0, has_side_effects=True, vmem_limit_bytes=56 * 2**20
        ),
        cost_estimate=pl.CostEstimate(flops=2 * 2048 * 1024 * 1536, bytes_accessed=20 * 2**20, transcendentals=0),
    )(tokens, gain, gate_weight, up_weight)


def gram(left, right):
    left = left.reshape(TOTAL, left.shape[-1])
    right = right.reshape(TOTAL, right.shape[-1])
    return lax.dot_general(
        left, right, (((0,), (0,)), ((), ())), preferred_element_type=F32
    ) / float(TOTAL)


def per_device(tokens, lang_ids, norm_gain, gate_weight, up_weight):
    masked = jnp.where((lang_ids == 0)[:, None], tokens, jnp.zeros_like(tokens))
    xf, xs, hf, hs = panels(masked, norm_gain.reshape(16, 1, FEAT), gate_weight, up_weight)
    return (gram(xf, xs), gram(hf, hs))


def solution(mesh):
    in_specs = (P("seq", "fsdp"), P("seq"), P(), P("seq", "fsdp"), P("seq", "fsdp"))
    out_specs = (P("fsdp", "seq"), P("fsdp", "seq"))
    return jax.shard_map(
        per_device, mesh=mesh, in_specs=in_specs, out_specs=out_specs, check_vma=False
    )
```

time: 619 us -> 209 us (0.34)
  waiting for transfers between devices: 554 us -> 0 us
  Pallas kernels: 0 us -> 187 us
  matrix products: 32.3 us -> 15.3 us
  between operations: 14.2 us -> 0.65 us
  other arithmetic: 14.8 us -> 2.44 us
    all_gather x5 -> x0, waiting for transfers between devices: 380 us -> none  [the longest x1 123 us: per_device(): lax.all_gather(gate_weight, 'seq', axis=0, tiled=True)]
    pallas_call x0 -> x1, Pallas kernels: none -> 187 us  [panels(): pl.pallas_call(kernel, out_shape=[jax.ShapeDtypeStruct(shape, BF16) for s...]
    psum x1 -> x0, waiting for transfers between devices: 172 us -> none  [spread(): return lax.psum(jnp.where(mine, shard, jnp.zeros_like(shard)), axis)]
    dot_general x4 -> x2, matrix products: 32.3 us -> 15.3 us  [gram(): lax.dot_general(left, right, (((0,), (0,)), ((), ())), preferred_element_...]
    select_n x2 -> x1, other arithmetic: 8.87 us -> 1.76 us  [per_device(): masked = jnp.where((lang_ids == 0)[:, None], tokens, jnp.zeros_like(tokens))]
  transfers between devices with their start and end apart: 6 -> 0, of which waited for: 6 -> 0; matrix products, arithmetic and copies ran while one was open for 5% -> 0% of each run, Pallas kernels for 0% -> 0%
where the time goes in v1:
time: 209 us; the launch traced here: 206 us
  Pallas kernels  187 us (89%)
  matrix products  15.3 us (7%)
  other arithmetic  2.44 us (1%)
    pallas_call x1, Pallas kernels, panels(): pl.pallas_call(kernel, out_shape=[jax.ShapeDtypeStruct(shape, BF16) for s...  187 us
    dot_general x2, matrix products, gram(): lax.dot_general(left, right, (((0,), (0,)), ((), ())), preferred_element_...  15.3 us

profile of v1, /device:TPU:1, one launch (start us, length us, event | category | flops | bytes accessed | tf_op | source)
XLA Modules:
  0.0 205.8 jit_solution(7166648267801741218)
XLA Ops:
  0.6 0.7 broadcast_compare_fusion
  1.3 1.8 broadcast_select_fusion.tok_ref
  3.1 187.4 %shard_map.68 = (bf16[4,2,256,512]{3,2,1,0:T(8,128)(2,1)}, bf16[4,2,256,1024]{3,2,1,0:T(8,128)(2,1)}, bf16[4,2,256,768]{3,2,1,0:T(8,128)(2,1)}, bf16[4,2,256,1536]{3,2,1,0:T(8,128)(2,1)}) custom-call(bf16[256,512]{1,0:T(8,128)(2,1)} %broadcast_select_fusion.tok_ref, f32[16,1,512]{2,1,0:T(1,128)} %bitcast.13, bf16[1024,768]{1,0:T(8,128)(2,1)} %wg_hbm.1, ...), custom_call_target="tpu_custom_call" | custom-call | flops 6442450944 | bytes 20971520 | tf_op jit(solution)/shard_map/pallas_call | solution.py:321
  190.5 0.0 copy-start
  190.5 6.6 %bitcast_multiply_fusion.1 = f32[512,1024]{1,0:T(8,128)} fusion(bf16[4,2,256,512]{3,2,1,0:T(8,128)(2,1)} %get-tuple-element.6, bf16[4,2,256,1024]{3,2,1,0:T(8,128)(2,1)} %get-tuple-element.7), kind=kOutput, calls=%fused_computation.1 | convolution fusion | flops 2148007936 | bytes 8388608 | tf_op jit(solution)/shard_map/dot_general | solution.py:337
  197.2 0.0 copy-done
  197.2 8.7 %bitcast_multiply_fusion = f32[768,1536]{1,0:T(8,128)} fusion(bf16[4,2,256,768]{3,2,1,0:T(8,128)(2,1)} %get-tuple-element.8, bf16[4,2,256,1536]{3,2,1,0:T(8,128)(2,1)S(1)} %copy-done), kind=kOutput, calls=%fused_computation | convolution fusion | flops 4833017856 | bytes 14155776 | tf_op jit(solution)/shard_map/dot_general | solution.py:337
Async XLA Ops:
  190.5 6.6 %copy-start = (bf16[4,2,256,1536]{3,2,1,0:T(8,128)(2,1)S(1)}, bf16[4,2,256,1536]{3,2,1,0:T(8,128)(2,1)}, u32[]{:S(2)}) copy-start(bf16[4,2,256,1536]{3,2,1,0:T(8,128)(2,1)} %get-tuple-element.9) | copy-start | bytes 18874372

commit v2 on v0

v2 whole, which is shorter than its diff:
```python
import jax
import jax.numpy as jnp
from jax import lax
from jax.experimental import pallas as pl
from jax.experimental.pallas import tpu as pltpu
from jax.sharding import PartitionSpec as P

MESH = pl.DeviceIdType.MESH
F32 = jnp.float32
BF16 = jnp.bfloat16
TOK = 256
FEAT = 512
COLS = 768
WA, WB = 512, 256
DEPTH = 1024
TOTAL = 2048
D = 8192
NH = 4
R = TOK // NH
ORDER = (
    "ZW:0", "ZW:1", "SC:0", "ZW:2", "SC:1", "R2:0", "C2:0", "ZW:3", "SC:2", "R2:1", "R3:0", "P:0:0", "SC:3",
    "C3:0:1", "C2:1", "C3:0:3", "P:0:1", "C3:0:2", "R2:2", "P:1:0", "C2:2", "P:0:3", "S:0:0", "P:0:2", "C3:1:1",
    "C3:1:3", "S:0:1", "C2:3", "P:2:0", "C3:1:2", "P:1:1", "P:1:3", "P:3:0", "S:1:0", "C3:2:1", "P:1:2",
    "C3:2:3", "S:0:3", "R3:1", "R2:3", "R3:2", "GX:0", "C3:2:2", "P:2:1", "S:0:2", "P:2:3", "P:2:2", "S:2:0",
    "SB:0", "S:1:1", "C3:3:1", "C3:3:3", "S:1:3", "P:3:1", "C3:3:2", "P:3:3", "S:3:0", "P:3:2", "S:1:2", "GX:1",
    "SB:1", "R3:3", "GX:2", "S:2:1", "S:2:3", "SB:2", "S:2:2", "HID:0", "S:3:1", "SB:3", "S:3:3", "S:3:2",
    "HID:1", "GX:3", "HID:2", "HZ:0", "HR2:0", "HID:3", "HZ:1", "HR2:1", "HZ:2", "HR2:2", "HR3:0", "HC2:0",
    "HR3:1", "HR3:2", "HC3:0:1", "HZ:3", "HR2:3", "HC3:0:3", "HC2:1", "HC3:0:2", "HR3:3", "HC3:1:1", "HC3:1:3",
    "HC2:2", "HL:0", "HC3:1:2", "HC3:2:1", "HL:1", "HC3:2:3", "HC2:3", "HC3:2:2", "HC3:3:1", "HL:2", "HC3:3:3",
    "HC3:3:2", "HL:3",
)

_RANGES = {}
_next = 0
for _name, _count in (
    ("z", 3), ("ss", 8), ("rsa", 4), ("rsb", 4), ("rsa2", 4), ("rsb2", 1),
    ("Xcy", 4), ("Xrx", 4), ("Xax", 4), ("Xsib", 4), ("Xrz", 4),
    ("Hz", 3), ("Hcy", 4), ("Hrx", 4), ("Hax", 4), ("Hsib", 4), ("Hrz", 4),
):
    _RANGES[_name] = _next
    _next += _count
PER_PART = _next


def mod4(v):
    return lax.rem(v + 8, 4)


def kernel(
    tok_ref, lang_ref, gain_ref, wg_hbm, wu_hbm,
    gin_out, ghid_out,
    raw, nb, ss, scol, xc, xf, xs, wg, wu, pa, pb, ra, ra2, rb, rb2, sbf,
    hb, hc, hf, hs, xft, hft, gin, ghid,
    ssem, rsem, wsem, osem,
):
    f = lax.axis_index("fsdp")
    s = lax.axis_index("seq")
    zh, y, c = f // 8, lax.rem(f // 2, 4), lax.rem(f, 2)
    zl, x = s // 4, lax.rem(s, 4)

    def dev(zh_, y_, c_, zl_, x_):
        return (zh_ * 8 + y_ * 2 + c_, zl_ * 4 + x_)

    z_src = [(zh, 1 - zl), (1 - zh, zl), (1 - zh, 1 - zl)]
    z_peers = [dev(a, y, c, b, x) for a, b in z_src]
    partner = z_peers[0]
    sib = dev(zh, y, 1 - c, zl, x)

    def x_peer(d):
        return dev(zh, y, c, zl, mod4(x + d))

    def y_peer(d, e=0):
        return dev(zh, mod4(y + d), c if e == 0 else 1 - c, zl, x)

    pending = []
    outs = []

    def remote(src, dst, h, name, i, device):
        at = h * PER_PART + _RANGES[name] + i
        return pltpu.make_async_remote_copy(
            src_ref=src, dst_ref=dst, send_sem=ssem.at[at], recv_sem=rsem.at[at],
            device_id=device, device_id_type=MESH,
        )

    def send(src, dst, h, name, i, device):
        copy = remote(src, dst, h, name, i, device)
        copy.start()
        pending.append(copy)

    def arrived(dst, h, name, i):
        remote(dst, dst, h, name, i, sib).wait_recv()

    w_copies = [
        pltpu.make_async_copy(wg_hbm, wg, wsem.at[0]),
        pltpu.make_async_copy(wu_hbm, wu, wsem.at[1]),
    ]
    for copy in w_copies:
        copy.start()

    barrier = pltpu.get_barrier_semaphore()
    peers = list(z_peers) + [x_peer(d) for d in (1, 2, 3)]
    peers += [y_peer(d, e) for d in range(4) for e in range(2) if (d, e) != (0, 0)]
    for peer in peers:
        pl.semaphore_signal(barrier, inc=1, device_id=peer, device_id_type=MESH)
    keep = (lang_ref[...] == 0).astype(F32)
    for i in range(TOK // 128):
        col = jnp.transpose(jnp.broadcast_to(keep[i:i + 1], (128, 128)))
        for k in range(FEAT // 128):
            lanes = slice(k * 128, (k + 1) * 128)
            v = (tok_ref[i * 128:(i + 1) * 128, lanes].astype(F32) * col).astype(BF16)
            for j in range(128 // R):
                raw[i * (128 // R) + j, zh, zl, :, lanes] = v[j * R:(j + 1) * R]
    pl.semaphore_wait(barrier, len(peers))

    def z_send(h, name, own):
        for i, peer in enumerate(z_peers):
            send(own.at[h, zh, zl], own.at[h, zh, zl], h, name, i, peer)

    def z_wait(h, name, own):
        for i, (a, b) in enumerate(z_src):
            arrived(own.at[h, a, b], h, name, i)

    slot = y * 2 + c

    def squares(h):
        v0 = raw[h, 0].reshape(2 * R, FEAT).astype(F32)
        v1 = raw[h, 1].reshape(2 * R, FEAT).astype(F32)
        sq = v0 * v0 + v1 * v1
        sq = sq[:, 0:128] + sq[:, 128:256] + sq[:, 256:384] + sq[:, 384:512]
        row = jnp.sum(jnp.transpose(sq), axis=0, keepdims=True)
        ss[h, slot] = jnp.broadcast_to(row, (8, 2 * R))
        for d in range(4):
            for e in range(2):
                if (d, e) != (0, 0):
                    send(ss.at[h, slot], ss.at[h, slot], h, "ss", d * 2 + e, y_peer(d, e))

    def scales(h):
        for d in range(4):
            for e in range(2):
                if (d, e) != (0, 0):
                    at = mod4(y - d) * 2 + (c if e == 0 else 1 - c)
                    arrived(ss.at[h, at], h, "ss", d * 2 + e)
        total = ss[h, 0]
        for i in range(1, 8):
            total = total + ss[h, i]
        scale = lax.rsqrt(total / float(D) + 1e-05)
        scol[h] = jnp.transpose(jnp.broadcast_to(scale[0:1], (128, 2 * R)))

    def normalize(h, src, dst, b, yy):
        g = gain_ref[b * 8 + yy * 2 + c]
        col = scol[h]
        for k in range(FEAT // 128):
            lanes = slice(k * 128, (k + 1) * 128)
            v = src[:, :, lanes].reshape(2 * R, 128).astype(F32)
            dst[:, :, lanes] = (v * col * g[:, lanes]).astype(BF16).reshape(2, R, 128)

    def row_first(h, q, own, row):
        for d in (1, 3):
            send(own.at[zl], row.at[h, x, zl], h, q + "rx", d, x_peer(d))

    def column_first(h, q, own, col):
        for d in (1, 3, 2):
            send(own.at[h, zl], col.at[h, y], h, q + "cy", d, y_peer(d))
        col[h, y] = own[h, zl]

    def column_wait(h, q, col, yy):
        d = mod4(y - yy)

        @pl.when(d != 0)
        def _():
            arrived(col.at[h, yy], h, q + "cy", d)

        if q == "X":
            normalize(h, col.at[h, yy], col.at[h, yy], zl, yy)

    def column_second(h, q, col, panel):
        for d in (1, 3, 2):
            to = mod4(x + d)
            column_wait(h, q, col, to)
            send(col.at[h, to], panel.at[h, c, x], h, q + "ax", d, x_peer(d))
        column_wait(h, q, col, x)
        send(col.at[h, x], panel.at[h, c, x], h, q + "sib", 0, sib)
        panel[h, c, x] = col[h, x]

    def column_third(h, q, panel, d):
        at = mod4(x - d)
        arrived(panel.at[h, c, at], h, q + "ax", d)
        send(panel.at[h, c, at], panel.at[h, c, at], h, q + "sib", d, sib)

    def column_done(h, q, panel, d):
        arrived(panel.at[h, 1 - c, mod4(x - d)], h, q + "sib", d)

    def row_second(h, q, own, row):
        row[h, x] = own[...]
        for d, half in ((1, 0), (3, 1)):
            at = mod4(x - d)
            arrived(row.at[h, at, zl], h, q + "rx", d)
            rows = pl.ds(half * (R // 2), R // 2)
            send(row.at[h, at, zl, rows], row.at[h, at, zl, rows], h, q + "rx", 2 * half, x_peer(d))
            send(row.at[h, at, zl], row.at[h, at, zl], h, q + "rz", d, partner)

    def row_third(h, q, row):
        at = mod4(x - 2)
        for half in range(2):
            arrived(row.at[h, at, zl, pl.ds(half * (R // 2), R // 2)], h, q + "rx", 2 * half)
        send(row.at[h, at, zl], row.at[h, at, zl], h, q + "rz", 2, partner)

    def row_done(h, q, row):
        for d in (1, 3, 2):
            arrived(row.at[h, mod4(x - d), 1 - zl], h, q + "rz", d)

    def products(h, d):
        column_done(h, "X", xs, d)
        at = mod4(x - d)
        a0 = xs[h, 0, at].reshape(2 * R, FEAT)
        a1 = xs[h, 1, at].reshape(2 * R, FEAT)

        def product(w, lanes):
            v = jnp.dot(a0, w[0:FEAT, lanes], preferred_element_type=F32)
            v = v + jnp.dot(a1, w[FEAT:DEPTH, lanes], preferred_element_type=F32)
            return v.astype(BF16).reshape(2, R, 256)

        def step(n, _):
            here = pl.ds(pl.multiple_of(n * 256, 256), 256)
            there = pl.ds(pl.multiple_of(WA + n * 256, 256), 256)
            pa[h, at, :, :, here] = product(wg, here)
            pa[h, at, :, :, there] = product(wu, here)
            return 0

        lax.fori_loop(0, WA // 256, step, 0)
        send(pa.at[h, at, 1 - zl], ra.at[h, at], h, "rsa", d, partner)
        pb[h, at, :, :, 0:WB] = product(wg, slice(WA, COLS))
        pb[h, at, :, :, WB:2 * WB] = product(wu, slice(WA, COLS))
        if d:
            send(pb.at[h, at], rb.at[h, x], h, "rsb", 4 - d, dev(zh, y, c, zl, at))

    def second(h, d):
        at = mod4(x - d)
        arrived(ra.at[h, at], h, "rsa", d)
        if d:
            pa[h, at, zl] = (pa[h, at, zl].astype(F32) + ra[h, at].astype(F32)).astype(BF16)
            send(pa.at[h, at, zl], ra2.at[h, x], h, "rsa2", 4 - d, dev(zh, y, c, zl, at))

    def swiglu(v, w):
        g, u = v[:, 0:w], v[:, w:2 * w]
        return (g / (1.0 + jnp.exp(-g)) * u).astype(BF16)

    def sum_b(h, t):
        v = pb[h, x, t].astype(F32)
        for d in (1, 2, 3):
            v = v + rb[h, mod4(x - d), t].astype(F32)
        return v

    def second_b(h):
        for d in (1, 3, 2):
            arrived(rb.at[h, mod4(x - d)], h, "rsb", d)
        sbf[h] = sum_b(h, 1 - zl).astype(BF16)
        send(sbf.at[h], rb2.at[h], h, "rsb2", 0, partner)

    def hidden(h):
        arrived(rb2.at[h], h, "rsb2", 0)
        hb[h, zh, zl, :, WA:COLS] = swiglu(sum_b(h, zl) + rb2[h].astype(F32), WB)
        for d in (1, 3, 2):
            arrived(ra2.at[h, mod4(x - d)], h, "rsa2", d)
        va = pa[h, x, zl].astype(F32) + ra[h, x].astype(F32)
        for d in (1, 2, 3):
            va = va + ra2[h, mod4(x - d)].astype(F32)
        hb[h, zh, zl, :, 0:WA] = swiglu(va, WA)

    def gram(h, row, flipped, panel, total, w):
        def flip(i, _):
            lanes = pl.ds(pl.multiple_of(i * 2 * R, 2 * R), 2 * R)
            flipped[:, lanes] = jnp.transpose(row[h, i].reshape(2 * R, w))
            return 0

        lax.fori_loop(0, 4, flip, 0)

        def step(i, _):
            cc, n = i // (w // 256), lax.rem(i, w // 256)
            here = pl.ds(pl.multiple_of(n * 256, 256), 256)
            there = pl.ds(pl.multiple_of(i * 256, 256), 256)
            right = panel[h, cc, :, :, :, here].reshape(8 * R, 256)
            v = jnp.dot(flipped[...], right, preferred_element_type=F32) * (1.0 / TOTAL)
            if h:
                v = v + total[:, there]
            total[:, there] = v
            return 0

        lax.fori_loop(0, 2 * w // 256, step, 0)

    def store(src, dst):
        copy = pltpu.make_async_copy(src, dst, osem.at[len(outs)])
        copy.start()
        outs.append(copy)

    def step_zw(h):
        z_wait(h, "z", raw)
        if h + 2 < NH:
            z_send(h + 2, "z", raw)
        column_first(h, "X", raw, xc)
        squares(h)

    def step_sc(h):
        scales(h)
        normalize(h, raw.at[h, zh], nb.at[h], zh, y)
        row_first(h, "X", nb.at[h], xf)

    def step_p(h, d):
        if (h, d) == (0, 0):
            for copy in w_copies:
                copy.wait()
        products(h, d)

    def step_hid(h):
        hidden(h)
        z_send(h, "Hz", hb)
        row_first(h, "H", hb.at[h, zh], hf)

    def step_hz(h):
        z_wait(h, "Hz", hb)
        column_first(h, "H", hb, hc)

    def step_hl(h):
        for d in (0, 1, 3, 2):
            column_done(h, "H", hs, d)
        row_done(h, "H", hf)
        gram(h, hf, hft, hs, ghid, COLS)

    def step_gx(h):
        row_done(h, "X", xf)
        gram(h, xf, xft, xs, gin, FEAT)
        if h == NH - 1:
            store(gin, gin_out)

    named = {
        "ZW": step_zw,
        "SC": step_sc,
        "C2": lambda h: column_second(h, "X", xc, xs),
        "C3": lambda h, d: column_third(h, "X", xs, d),
        "P": step_p,
        "R2": lambda h: row_second(h, "X", nb.at[h], xf),
        "R3": lambda h: row_third(h, "X", xf),
        "S": second,
        "SB": second_b,
        "HID": step_hid,
        "HZ": step_hz,
        "HC2": lambda h: column_second(h, "H", hc, hs),
        "HR2": lambda h: row_second(h, "H", hb.at[h, zh], hf),
        "HR3": lambda h: row_third(h, "H", hf),
        "HC3": lambda h, d: column_third(h, "H", hs, d),
        "HL": step_hl,
        "GX": step_gx,
    }
    for h in range(min(2, NH)):
        z_send(h, "z", raw)
    for step in ORDER:
        name, *places = step.split(":")
        named[name](*[int(place) for place in places])
    store(ghid, ghid_out)
    for copy in pending:
        copy.wait_send()
    for copy in outs:
        copy.wait()


def grams(tokens, lang, gain, gate_weight, up_weight):
    def vm(*shape, dtype=BF16):
        return pltpu.VMEM(shape, dtype)

    any_spec = pl.BlockSpec(memory_space=pl.ANY)
    vmem_spec = pl.BlockSpec(memory_space=pltpu.VMEM)
    scratch = [
        vm(NH, 2, 2, R, FEAT), vm(NH, 2, R, FEAT), vm(NH, 8, 8, 2 * R, dtype=F32), vm(NH, 2 * R, 128, dtype=F32),
        vm(NH, 4, 2, R, FEAT), vm(NH, 4, 2, R, FEAT), vm(NH, 2, 4, 2, R, FEAT),
        vm(DEPTH, COLS), vm(DEPTH, COLS),
        vm(NH, 4, 2, R, 2 * WA), vm(NH, 4, 2, R, 2 * WB),
        vm(NH, 4, R, 2 * WA), vm(NH, 4, R, 2 * WA),
        vm(NH, 4, 2, R, 2 * WB), vm(NH, R, 2 * WB), vm(NH, R, 2 * WB),
        vm(NH, 2, 2, R, COLS), vm(NH, 4, 2, R, COLS), vm(NH, 4, 2, R, COLS), vm(NH, 2, 4, 2, R, COLS),
        vm(FEAT, 8 * R), vm(COLS, 8 * R),
        vm(FEAT, 2 * FEAT, dtype=F32), vm(COLS, 2 * COLS, dtype=F32),
        pltpu.SemaphoreType.DMA((NH * PER_PART,)), pltpu.SemaphoreType.DMA((NH * PER_PART,)),
        pltpu.SemaphoreType.DMA((2,)), pltpu.SemaphoreType.DMA((2,)),
    ]
    return pl.pallas_call(
        kernel,
        out_shape=[
            jax.ShapeDtypeStruct((FEAT, 2 * FEAT), F32),
            jax.ShapeDtypeStruct((COLS, 2 * COLS), F32),
        ],
        in_specs=[vmem_spec, vmem_spec, vmem_spec, any_spec, any_spec],
        out_specs=[any_spec] * 2,
        scratch_shapes=scratch,
        compiler_params=pltpu.CompilerParams(
            collective_id=0, has_side_effects=True, vmem_limit_bytes=60 * 2**20
        ),
        cost_estimate=pl.CostEstimate(flops=13 * 10**9, bytes_accessed=10 * 2**20, transcendentals=0),
    )(tokens, lang, gain, gate_weight, up_weight)


def per_device(tokens, lang_ids, norm_gain, gate_weight, up_weight):
    gain = norm_gain.reshape(16, 1, FEAT)
    return tuple(grams(tokens, lang_ids.reshape(TOK // 128, 128), gain, gate_weight, up_weight))


def solution(mesh):
    in_specs = (P("seq", "fsdp"), P("seq"), P(), P("seq", "fsdp"), P("seq", "fsdp"))
    out_specs = (P("fsdp", "seq"), P("fsdp", "seq"))
    return jax.shard_map(
        per_device, mesh=mesh, in_specs=in_specs, out_specs=out_specs, check_vma=False
    )
```

time: 619 us -> 176 us (0.28)
  waiting for transfers between devices: 554 us -> 0 us
  Pallas kernels: 0 us -> 166 us
  matrix products: 32.3 us -> 0 us
  other arithmetic: 14.8 us -> 0 us
  between operations: 14.2 us -> 0.64 us
    all_gather x5 -> x0, waiting for transfers between devices: 380 us -> none  [the longest x1 123 us: per_device(): lax.all_gather(gate_weight, 'seq', axis=0, tiled=True)]
    psum x1 -> x0, waiting for transfers between devices: 172 us -> none  [spread(): return lax.psum(jnp.where(mine, shard, jnp.zeros_like(shard)), axis)]
    pallas_call x0 -> x1, Pallas kernels: none -> 166 us  [grams(): pl.pallas_call(kernel, out_shape=[jax.ShapeDtypeStruct((FEAT, 2 * FEAT),...]
    dot_general x4 -> x0, matrix products: 32.3 us -> none  [the longest x2 13.4 us: tile_gram(): jnp.einsum('ti,tj->ij', left, right, preferred_element_type=jnp.float32)]
    select_n x2 -> x0, other arithmetic: 8.87 us -> none  [spread(): return lax.psum(jnp.where(mine, shard, jnp.zeros_like(shard)), axis)]
  transfers between devices with their start and end apart: 6 -> 0, of which waited for: 6 -> 0; matrix products, arithmetic and copies ran while one was open for 5% -> 0% of each run, Pallas kernels for 0% -> 0%
where the time goes in v2:
time: 176 us; the launch traced here: 175 us
  Pallas kernels  166 us (94%)
  local copies, waits for them, and re-layouts  8 us (5%)
    pallas_call x1, Pallas kernels, grams(): pl.pallas_call(kernel, out_shape=[jax.ShapeDtypeStruct((FEAT, 2 * FEAT),...  166 us
    unnamed x2, local copies, waits for them, and re-layouts  8 us

profile of v2, /device:TPU:1, one launch (start us, length us, event | category | flops | bytes accessed | tf_op | source)
XLA Modules:
  0.0 174.5 jit_solution(9454194026992457803)
XLA Ops:
  0.6 165.9 %shard_map.68 = (f32[512,1024]{1,0:T(8,128)}, f32[768,1536]{1,0:T(8,128)}) custom-call(bf16[256,512]{1,0:T(8,128)(2,1)} %tok_ref.1, s32[2,128]{1,0:T(2,128)} %bitcast.3, f32[16,1,512]{2,1,0:T(1,128)} %bitcast.2, bf16[1024,768]{1,0:T(8,128)(2,1)} %wg_hbm.1, bf16[1024,768]{1,0:T(8,128)(2,1)} %wu_hbm.1), custom_call_target="tpu_custom_call" | custom-call | flops 12999999488 | bytes 10485760 | tf_op jit(solution)/shard_map/pallas_call | solution.py:385
  166.5 3.2 %copy.9 = f32[512,1024]{1,0:T(8,128)} copy(f32[512,1024]{1,0:T(8,128)} %get-tuple-element.4) | data formatting | bytes 4194304
  169.7 4.8 %copy.10 = f32[768,1536]{1,0:T(8,128)} copy(f32[768,1536]{1,0:T(8,128)} %get-tuple-element.5) | data formatting | bytes 9437184

commit v3 on v2

--- a/solution.py
+++ b/solution.py
@@ -18,22 +18,23 @@
 NH = 4
 R = TOK // NH
 ORDER = (
-    "ZW:0", "ZW:1", "SC:0", "ZW:2", "SC:1", "R2:0", "C2:0", "ZW:3", "SC:2", "R2:1", "R3:0", "P:0:0", "SC:3",
-    "C3:0:1", "C2:1", "C3:0:3", "P:0:1", "C3:0:2", "R2:2", "P:1:0", "C2:2", "P:0:3", "S:0:0", "P:0:2", "C3:1:1",
-    "C3:1:3", "S:0:1", "C2:3", "P:2:0", "C3:1:2", "P:1:1", "P:1:3", "P:3:0", "S:1:0", "C3:2:1", "P:1:2",
-    "C3:2:3", "S:0:3", "R3:1", "R2:3", "R3:2", "GX:0", "C3:2:2", "P:2:1", "S:0:2", "P:2:3", "P:2:2", "S:2:0",
-    "SB:0", "S:1:1", "C3:3:1", "C3:3:3", "S:1:3", "P:3:1", "C3:3:2", "P:3:3", "S:3:0", "P:3:2", "S:1:2", "GX:1",
-    "SB:1", "R3:3", "GX:2", "S:2:1", "S:2:3", "SB:2", "S:2:2", "HID:0", "S:3:1", "SB:3", "S:3:3", "S:3:2",
-    "HID:1", "GX:3", "HID:2", "HZ:0", "HR2:0", "HID:3", "HZ:1", "HR2:1", "HZ:2", "HR2:2", "HR3:0", "HC2:0",
-    "HR3:1", "HR3:2", "HC3:0:1", "HZ:3", "HR2:3", "HC3:0:3", "HC2:1", "HC3:0:2", "HR3:3", "HC3:1:1", "HC3:1:3",
-    "HC2:2", "HL:0", "HC3:1:2", "HC3:2:1", "HL:1", "HC3:2:3", "HC2:3", "HC3:2:2", "HC3:3:1", "HL:2", "HC3:3:3",
-    "HC3:3:2", "HL:3",
+    "ZN:0", "RX:3", "ZA:0", "Y:0", "ZN:1", "RX:0", "SC:0", "ZN:3", "RX:1", "R2:0", "ZN:2", "ZA:1", "Y:1", "RX:2",
+    "R2:1", "C2:0", "ZA:3", "Y:3", "SC:1", "R2:3", "R3:0", "C2:1", "ZA:2", "C3:0:1", "C3:0:3", "P:0:0", "Y:2",
+    "P:0:1", "C3:0:2", "SC:3", "P:0:3", "C2:3", "P:1:0", "C3:1:2", "C3:1:1", "P:1:1", "P:0:2", "P:3:0", "C3:1:3",
+    "SC:2", "C2:2", "SB:0", "C3:3:1", "P:2:0", "S:1:0", "S:0:3", "S:0:2", "P:1:2", "S:0:1", "C3:2:1", "P:1:3",
+    "S:0:0", "C3:2:2", "C3:3:2", "S:3:0", "P:2:1", "C3:2:3", "P:2:2", "S:1:3", "S:1:1", "S:1:2", "P:2:3",
+    "HID:0", "P:3:2", "S:2:2", "S:2:3", "R2:2", "SB:1", "HR1:0", "S:2:0", "S:2:1", "S:3:2", "HZ:0", "P:3:1",
+    "HID:1", "HR1:1", "GX:0", "R3:1", "C3:3:3", "P:3:3", "SB:2", "S:3:1", "HC2:0", "HR2:0", "HZ:1", "HID:2",
+    "S:3:3", "GX:1", "HC2:1", "SB:3", "HR3:0", "HR1:2", "HID:3", "HC3:0:3", "R3:2", "HZ:2", "HC3:0:1", "HR1:3",
+    "HC3:1:1", "HR2:1", "HZ:3", "HR2:2", "HC2:2", "R3:3", "HC3:0:2", "HR3:1", "GX:2", "HR2:3", "HL:0", "HC2:3",
+    "HC3:1:3", "HR3:2", "HC3:2:1", "HC3:2:3", "HC3:1:2", "HC3:2:2", "GX:3", "HL:1", "HC3:3:3", "HC3:3:1",
+    "HR3:3", "HC3:3:2", "HL:2", "HL:3",
 )
 
 _RANGES = {}
 _next = 0
 for _name, _count in (
-    ("z", 3), ("ss", 8), ("rsa", 4), ("rsb", 4), ("rsa2", 4), ("rsb2", 1),
+    ("z", 3), ("ss", 8), ("sx", 4), ("rsa", 4), ("rsb", 4), ("rsa2", 4), ("rsb2", 1),
     ("Xcy", 4), ("Xrx", 4), ("Xax", 4), ("Xsib", 4), ("Xrz", 4),
     ("Hz", 3), ("Hcy", 4), ("Hrx", 4), ("Hax", 4), ("Hsib", 4), ("Hrz", 4),
 ):
@@ -48,8 +49,8 @@
 
 def kernel(
     tok_ref, lang_ref, gain_ref, wg_hbm, wu_hbm,
-    gin_out, ghid_out,
-    raw, nb, ss, scol, xc, xf, xs, wg, wu, pa, pb, ra, ra2, rb, rb2, sbf,
+    gin_out, ghid_out, left_out, right_out,
+    raw, ss, srow, xc, xf, xs, wg, wu, pa, pb, ra, ra2, rb, rb2, sbf,
     hb, hc, hf, hs, xft, hft, gin, ghid,
     ssem, rsem, wsem, osem,
 ):
@@ -85,7 +86,13 @@
     def send(src, dst, h, name, i, device):
         copy = remote(src, dst, h, name, i, device)
         copy.start()
-        pending.append(copy)
+        pending.append((h, name, copy))
+
+    def sent(h=None, name=None):
+        for entry in list(pending):
+            if name is None or entry[:2] == (h, name):
+                entry[2].wait_send()
+                pending.remove(entry)
 
     def arrived(dst, h, name, i):
         remote(dst, dst, h, name, i, sib).wait_recv()
@@ -143,27 +150,30 @@
         total = ss[h, 0]
         for i in range(1, 8):
             total = total + ss[h, i]
-        scale = lax.rsqrt(total / float(D) + 1e-05)
-        scol[h] = jnp.transpose(jnp.broadcast_to(scale[0:1], (128, 2 * R)))
-
-    def normalize(h, src, dst, b, yy):
+        srow[h, x] = lax.rsqrt(total / float(D) + 1e-05)
+        for d in (1, 3, 2):
+            send(srow.at[h, x], srow.at[h, x], h, "sx", d, x_peer(d))
+
+    def scale_columns(h, xx):
+        return jnp.transpose(jnp.broadcast_to(srow[h, xx, 0:1], (128, 2 * R)))
+
+    def normalize(part, col, b, yy):
         g = gain_ref[b * 8 + yy * 2 + c]
-        col = scol[h]
         for k in range(FEAT // 128):
             lanes = slice(k * 128, (k + 1) * 128)
-            v = src[:, :, lanes].reshape(2 * R, 128).astype(F32)
-            dst[:, :, lanes] = (v * col * g[:, lanes]).astype(BF16).reshape(2, R, 128)
+            v = part[:, :, lanes].reshape(2 * R, 128).astype(F32)
+            part[:, :, lanes] = (v * col * g[:, lanes]).astype(BF16).reshape(2, R, 128)
 
     def row_first(h, q, own, row):
         for d in (1, 3):
-            send(own.at[zl], row.at[h, x, zl], h, q + "rx", d, x_peer(d))
+            send(own.at[h, zh, zl], row.at[h, x, zl], h, q + "rx", d, x_peer(d))
 
     def column_first(h, q, own, col):
         for d in (1, 3, 2):
             send(own.at[h, zl], col.at[h, y], h, q + "cy", d, y_peer(d))
         col[h, y] = own[h, zl]
 
-    def column_wait(h, q, col, yy):
+    def column_wait(h, q, col, yy, scale):
         d = mod4(y - yy)
 
         @pl.when(d != 0)
@@ -171,14 +181,15 @@
             arrived(col.at[h, yy], h, q + "cy", d)
 
         if q == "X":
-            normalize(h, col.at[h, yy], col.at[h, yy], zl, yy)
+            normalize(col.at[h, yy], scale, zl, yy)
 
     def column_second(h, q, col, panel):
+        scale = scale_columns(h, x) if q == "X" else None
         for d in (1, 3, 2):
             to = mod4(x + d)
-            column_wait(h, q, col, to)
+            column_wait(h, q, col, to, scale)
             send(col.at[h, to], panel.at[h, c, x], h, q + "ax", d, x_peer(d))
-        column_wait(h, q, col, x)
+        column_wait(h, q, col, x, scale)
         send(col.at[h, x], panel.at[h, c, x], h, q + "sib", 0, sib)
         panel[h, c, x] = col[h, x]
 
@@ -191,7 +202,7 @@
         arrived(panel.at[h, 1 - c, mod4(x - d)], h, q + "sib", d)
 
     def row_second(h, q, own, row):
-        row[h, x] = own[...]
+        row[h, x] = own[h, zh]
         for d, half in ((1, 0), (3, 1)):
             at = mod4(x - d)
             arrived(row.at[h, at, zl], h, q + "rx", d)
@@ -274,6 +285,11 @@
             return 0
 
         lax.fori_loop(0, 4, flip, 0)
+        if total is ghid and h == NH - 1:
+            store(flipped, left_out)
+            for cc in range(2):
+                store(panel.at[h, cc], right_out.at[:, :, :, pl.ds(cc * w, w)])
+            return
 
         def step(i, _):
             cc, n = i // (w // 256), lax.rem(i, w // 256)
@@ -287,23 +303,17 @@
             return 0
 
         lax.fori_loop(0, 2 * w // 256, step, 0)
+        if total is ghid and h == NH - 2:
+            store(ghid, ghid_out)
 
     def store(src, dst):
         copy = pltpu.make_async_copy(src, dst, osem.at[len(outs)])
         copy.start()
         outs.append(copy)
 
-    def step_zw(h):
+    def step_za(h):
         z_wait(h, "z", raw)
-        if h + 2 < NH:
-            z_send(h + 2, "z", raw)
-        column_first(h, "X", raw, xc)
         squares(h)
-
-    def step_sc(h):
-        scales(h)
-        normalize(h, raw.at[h, zh], nb.at[h], zh, y)
-        row_first(h, "X", nb.at[h], xf)
 
     def step_p(h, d):
         if (h, d) == (0, 0):
@@ -314,7 +324,6 @@
     def step_hid(h):
         hidden(h)
         z_send(h, "Hz", hb)
-        row_first(h, "H", hb.at[h, zh], hf)
 
     def step_hz(h):
         z_wait(h, "Hz", hb)
@@ -328,37 +337,44 @@
 
     def step_gx(h):
         row_done(h, "X", xf)
+        sent(h, "Xrx")
+        sent(h, "Xrz")
+        for d in (0, 1, 3, 2):
+            at = mod4(x - d)
+            if d:
+                arrived(srow.at[h, at], h, "sx", d)
+            normalize(xf.at[h, at], scale_columns(h, at), zh, y)
         gram(h, xf, xft, xs, gin, FEAT)
         if h == NH - 1:
             store(gin, gin_out)
 
     named = {
-        "ZW": step_zw,
-        "SC": step_sc,
+        "ZN": lambda h: z_send(h, "z", raw),
+        "RX": lambda h: row_first(h, "X", raw, xf),
+        "ZA": step_za,
+        "Y": lambda h: column_first(h, "X", raw, xc),
+        "SC": scales,
         "C2": lambda h: column_second(h, "X", xc, xs),
         "C3": lambda h, d: column_third(h, "X", xs, d),
         "P": step_p,
-        "R2": lambda h: row_second(h, "X", nb.at[h], xf),
+        "R2": lambda h: row_second(h, "X", raw, xf),
         "R3": lambda h: row_third(h, "X", xf),
         "S": second,
         "SB": second_b,
         "HID": step_hid,
+        "HR1": lambda h: row_first(h, "H", hb, hf),
         "HZ": step_hz,
         "HC2": lambda h: column_second(h, "H", hc, hs),
-        "HR2": lambda h: row_second(h, "H", hb.at[h, zh], hf),
+        "HR2": lambda h: row_second(h, "H", hb, hf),
         "HR3": lambda h: row_third(h, "H", hf),
         "HC3": lambda h, d: column_third(h, "H", hs, d),
         "HL": step_hl,
         "GX": step_gx,
     }
-    for h in range(min(2, NH)):
-        z_send(h, "z", raw)
     for step in ORDER:
         name, *places = step.split(":")
         named[name](*[int(place) for place in places])
-    store(ghid, ghid_out)
-    for copy in pending:
-        copy.wait_send()
+    sent()
     for copy in outs:
         copy.wait()
 
@@ -370,7 +386,7 @@
     any_spec = pl.BlockSpec(memory_space=pl.ANY)
     vmem_spec = pl.BlockSpec(memory_space=pltpu.VMEM)
     scratch = [
-        vm(NH, 2, 2, R, FEAT), vm(NH, 2, R, FEAT), vm(NH, 8, 8, 2 * R, dtype=F32), vm(NH, 2 * R, 128, dtype=F32),
+        vm(NH, 2, 2, R, FEAT), vm(NH, 8, 8, 2 * R, dtype=F32), vm(NH, 4, 8, 2 * R, dtype=F32),
         vm(NH, 4, 2, R, FEAT), vm(NH, 4, 2, R, FEAT), vm(NH, 2, 4, 2, R, FEAT),
         vm(DEPTH, COLS), vm(DEPTH, COLS),
         vm(NH, 4, 2, R, 2 * WA), vm(NH, 4, 2, R, 2 * WB),
@@ -380,16 +396,17 @@
         vm(FEAT, 8 * R), vm(COLS, 8 * R),
         vm(FEAT, 2 * FEAT, dtype=F32), vm(COLS, 2 * COLS, dtype=F32),
         pltpu.SemaphoreType.DMA((NH * PER_PART,)), pltpu.SemaphoreType.DMA((NH * PER_PART,)),
-        pltpu.SemaphoreType.DMA((2,)), pltpu.SemaphoreType.DMA((2,)),
+        pltpu.SemaphoreType.DMA((2,)), pltpu.SemaphoreType.DMA((5,)),
+    ]
+    shapes = [
+        ((FEAT, 2 * FEAT), F32), ((COLS, 2 * COLS), F32),
+        ((COLS, 8 * R), BF16), ((4, 2, R, 2 * COLS), BF16),
     ]
     return pl.pallas_call(
         kernel,
-        out_shape=[
-            jax.ShapeDtypeStruct((FEAT, 2 * FEAT), F32),
-            jax.ShapeDtypeStruct((COLS, 2 * COLS), F32),
-        ],
+        out_shape=[jax.ShapeDtypeStruct(shape, dtype) for shape, dtype in shapes],
         in_specs=[vmem_spec, vmem_spec, vmem_spec, any_spec, any_spec],
-        out_specs=[any_spec] * 2,
+        out_specs=[any_spec] * 4,
         scratch_shapes=scratch,
         compiler_params=pltpu.CompilerParams(
             collective_id=0, has_side_effects=True, vmem_limit_bytes=60 * 2**20
@@ -398,9 +415,36 @@
     )(tokens, lang, gain, gate_weight, up_weight)
 
 
+def last_kernel(gin, ghid, left, right, gin_out, ghid_out):
+    v = jnp.dot(left[...], right[...], preferred_element_type=F32) * (1.0 / TOTAL)
+    ghid_out[...] = ghid[...] + v
+    gin_out[...] = gin[...]
+
+
+def last_part(gin, ghid, left, right):
+    n = 8
+
+    def rows(a):
+        return pl.BlockSpec((a.shape[0] // n, a.shape[1]), lambda i: (i, 0))
+
+    return pl.pallas_call(
+        last_kernel,
+        grid=(n,),
+        out_shape=[jax.ShapeDtypeStruct(a.shape, F32) for a in (gin, ghid)],
+        in_specs=[rows(gin), rows(ghid), rows(left), pl.BlockSpec(right.shape, lambda i: (0, 0))],
+        out_specs=[rows(gin), rows(ghid)],
+        compiler_params=pltpu.CompilerParams(vmem_limit_bytes=60 * 2**20),
+        cost_estimate=pl.CostEstimate(
+            flops=2 * COLS * 2 * COLS * 8 * R, bytes_accessed=16 * 2**20, transcendentals=0
+        ),
+    )(gin, ghid, left, right)
+
+
 def per_device(tokens, lang_ids, norm_gain, gate_weight, up_weight):
     gain = norm_gain.reshape(16, 1, FEAT)
-    return tuple(grams(tokens, lang_ids.reshape(TOK // 128, 128), gain, gate_weight, up_weight))
+    lang = lang_ids.reshape(TOK // 128, 128)
+    gin, ghid, left, right = grams(tokens, lang, gain, gate_weight, up_weight)
+    return tuple(last_part(gin, ghid, left, right.reshape(8 * R, 2 * COLS)))
 
 
 def solution(mesh):

time: 176 us -> 162 us (0.920)
  local copies, waits for them, and re-layouts: 8 us -> 0 us
  Pallas kernels: 166 us -> 161 us
    unnamed x2 -> x0, local copies, waits for them, and re-layouts: 8 us -> none
    pallas_call x1 -> x2, Pallas kernels: 166 us -> 161 us  [the longest x1 151 us: grams(): pl.pallas_call(kernel, out_shape=[jax.ShapeDtypeStruct(shape, dtype) for...]
where the time goes in v3:
time: 162 us
  Pallas kernels  161 us (99%)
    pallas_call x1, Pallas kernels, grams(): pl.pallas_call(kernel, out_shape=[jax.ShapeDtypeStruct(shape, dtype) for...  151 us
    pallas_call x1, Pallas kernels, last_part(): pl.pallas_call(last_kernel, grid=(n,), out_shape=[jax.ShapeDtypeStruct(a....  9.85 us

profile of v3, /device:TPU:1, one launch (start us, length us, event | category | flops | bytes accessed | tf_op | source)
XLA Modules:
  0.0 161.5 jit_solution(13565636772386655930)
XLA Ops:
  0.6 151.0 %shard_map.68 = (f32[512,1024]{1,0:T(8,128)}, f32[768,1536]{1,0:T(8,128)}, bf16[768,512]{1,0:T(8,128)(2,1)}, bf16[4,2,64,1536]{3,2,1,0:T(8,128)(2,1)}) custom-call(bf16[256,512]{1,0:T(8,128)(2,1)} %tok_ref.1, s32[2,128]{1,0:T(2,128)} %bitcast.5, f32[16,1,512]{2,1,0:T(1,128)} %bitcast.4, bf16[1024,768]{1,0:T(8,128)(2,1)} %wg_hbm.1, bf16[1024,768]{1,0:T(8,128)(2,1)} %wu_hbm.1), custom_call_target="tpu_custom_call" | custom-call | flops 12999999488 | bytes 10485760 | tf_op jit(solution)/shard_map/pallas_call | solution.py:405
  151.7 9.9 %shard_map.69 = (f32[512,1024]{1,0:T(8,128)}, f32[768,1536]{1,0:T(8,128)}) custom-call(f32[512,1024]{1,0:T(8,128)} %get-tuple-element.6.gin, f32[768,1536]{1,0:T(8,128)} %get-tuple-element.7.ghid, bf16[768,512]{1,0:T(8,128)(2,1)} %get-tuple-element.8.left, bf16[512,1536]{1,0:T(8,128)(2,1)} %bitcast.3), custom_call_target="tpu_custom_call" | custom-call | flops 1207959552 | bytes 16777216 | tf_op jit(solution)/shard_map/pallas_call | solution.py:430

commit v4 on v3

--- a/solution.py
+++ b/solution.py
@@ -18,17 +18,17 @@
 NH = 4
 R = TOK // NH
 ORDER = (
-    "ZN:0", "RX:3", "ZA:0", "Y:0", "ZN:1", "RX:0", "SC:0", "ZN:3", "RX:1", "R2:0", "ZN:2", "ZA:1", "Y:1", "RX:2",
-    "R2:1", "C2:0", "ZA:3", "Y:3", "SC:1", "R2:3", "R3:0", "C2:1", "ZA:2", "C3:0:1", "C3:0:3", "P:0:0", "Y:2",
-    "P:0:1", "C3:0:2", "SC:3", "P:0:3", "C2:3", "P:1:0", "C3:1:2", "C3:1:1", "P:1:1", "P:0:2", "P:3:0", "C3:1:3",
-    "SC:2", "C2:2", "SB:0", "C3:3:1", "P:2:0", "S:1:0", "S:0:3", "S:0:2", "P:1:2", "S:0:1", "C3:2:1", "P:1:3",
-    "S:0:0", "C3:2:2", "C3:3:2", "S:3:0", "P:2:1", "C3:2:3", "P:2:2", "S:1:3", "S:1:1", "S:1:2", "P:2:3",
-    "HID:0", "P:3:2", "S:2:2", "S:2:3", "R2:2", "SB:1", "HR1:0", "S:2:0", "S:2:1", "S:3:2", "HZ:0", "P:3:1",
-    "HID:1", "HR1:1", "GX:0", "R3:1", "C3:3:3", "P:3:3", "SB:2", "S:3:1", "HC2:0", "HR2:0", "HZ:1", "HID:2",
-    "S:3:3", "GX:1", "HC2:1", "SB:3", "HR3:0", "HR1:2", "HID:3", "HC3:0:3", "R3:2", "HZ:2", "HC3:0:1", "HR1:3",
-    "HC3:1:1", "HR2:1", "HZ:3", "HR2:2", "HC2:2", "R3:3", "HC3:0:2", "HR3:1", "GX:2", "HR2:3", "HL:0", "HC2:3",
-    "HC3:1:3", "HR3:2", "HC3:2:1", "HC3:2:3", "HC3:1:2", "HC3:2:2", "GX:3", "HL:1", "HC3:3:3", "HC3:3:1",
-    "HR3:3", "HC3:3:2", "HL:2", "HL:3",
+    "ZN:0", "ZA:0", "ZN:2", "Y:0", "RX:2", "RX:1", "RX:3", "SC:0", "ZN:3", "ZA:2", "Y:2", "ZN:1", "RX:0", "R2:2",
+    "C2:0", "ZA:3", "R3:2", "Y:3", "R2:0", "SC:2", "ZA:1", "R2:1", "C2:2", "Y:1", "SC:3", "R3:0", "C3:0:3",
+    "C3:0:1", "P:0:0", "P:2:0", "C2:3", "P:0:3", "C3:0:2", "C3:2:1", "SC:1", "C2:1", "P:0:1", "C3:2:3", "C3:2:2",
+    "P:0:2", "P:2:1", "P:2:2", "C3:3:3", "C3:3:2", "P:2:3", "S:2:0", "PB:0", "C3:3:1", "C3:1:3", "S:0:1",
+    "P:1:0", "C3:1:2", "C3:1:1", "S:0:3", "S:0:2", "PB:2", "S:0:0", "P:1:3", "GX:0", "P:3:2", "SB:0", "P:1:1",
+    "S:2:2", "P:1:2", "S:2:3", "SA:0", "HID:0", "PB:1", "S:3:2", "P:3:3", "SB:2", "S:1:3", "S:1:2", "HR1:0",
+    "P:3:1", "S:1:1", "S:2:1", "SA:2", "PB:3", "HZ:0", "R3:1", "SA:1", "HID:2", "HR1:2", "S:1:0", "S:3:1",
+    "S:3:3", "P:3:0", "GX:1", "SB:1", "SA:3", "HZ:2", "R2:3", "HC2:0", "SB:3", "HID:1", "GX:2", "S:3:0", "HR1:1",
+    "HC2:2", "HID:3", "R3:3", "HZ:1", "HC3:0:2", "HR1:3", "HR2:2", "HR2:1", "HR2:0", "HZ:3", "GX:3", "HC2:1",
+    "HC3:2:3", "HR3:2", "HR3:0", "HC3:2:1", "HC3:0:3", "HC2:3", "HR3:1", "HC3:0:1", "HC3:1:3", "HR2:3",
+    "HC3:2:2", "HC3:1:1", "HC3:1:2", "HL:0", "HL:1", "HR3:3", "HC3:3:1", "HC3:3:3", "HC3:3:2", "HL:2", "HL:3",
 )
 
 _RANGES = {}
@@ -50,7 +50,7 @@
 def kernel(
     tok_ref, lang_ref, gain_ref, wg_hbm, wu_hbm,
     gin_out, ghid_out, left_out, right_out,
-    raw, ss, srow, xc, xf, xs, wg, wu, pa, pb, ra, ra2, rb, rb2, sbf,
+    raw, ss, srow, xc, xf, xs, wg, wu, pa, pf, pz, pb, ra, rah, ra2, rb, rbh, rb2, sbf,
     hb, hc, hf, hs, xft, hft, gin, ghid,
     ssem, rsem, wsem, osem,
 ):
@@ -229,28 +229,54 @@
         def product(w, lanes):
             v = jnp.dot(a0, w[0:FEAT, lanes], preferred_element_type=F32)
             v = v + jnp.dot(a1, w[FEAT:DEPTH, lanes], preferred_element_type=F32)
-            return v.astype(BF16).reshape(2, R, 256)
+            return v.reshape(2, R, 256)
+
+        def keep_a(v, lanes):
+            pf[h, at, :, lanes] = jnp.where(zl == 0, v[0], v[1])
+            pa[h, at, :, lanes] = jnp.where(zl == 0, v[1], v[0]).astype(BF16)
 
         def step(n, _):
             here = pl.ds(pl.multiple_of(n * 256, 256), 256)
             there = pl.ds(pl.multiple_of(WA + n * 256, 256), 256)
-            pa[h, at, :, :, here] = product(wg, here)
-            pa[h, at, :, :, there] = product(wu, here)
+            keep_a(product(wg, here), here)
+            keep_a(product(wu, here), there)
             return 0
 
         lax.fori_loop(0, WA // 256, step, 0)
-        send(pa.at[h, at, 1 - zl], ra.at[h, at], h, "rsa", d, partner)
-        pb[h, at, :, :, 0:WB] = product(wg, slice(WA, COLS))
-        pb[h, at, :, :, WB:2 * WB] = product(wu, slice(WA, COLS))
-        if d:
-            send(pb.at[h, at], rb.at[h, x], h, "rsb", 4 - d, dev(zh, y, c, zl, at))
+        send(pa.at[h, at], ra.at[h, at], h, "rsa", d, partner)
+        pb[h, at, :, :, 0:WB] = product(wg, slice(WA, COLS)).astype(BF16)
+        pb[h, at, :, :, WB:2 * WB] = product(wu, slice(WA, COLS)).astype(BF16)
+        if d == 2:
+            send(pb.at[h, at, 0], rbh.at[h, 0], h, "rsb", 2, x_peer(1))
+            send(pb.at[h, at, 1], rbh.at[h, 1], h, "rsb", 0, x_peer(3))
+
+    def pass_b(h):
+        for half, d in ((0, 1), (1, 3)):
+            at = mod4(x + d)
+            arrived(rbh.at[h, half], h, "rsb", 2 - 2 * half)
+            pb[h, at, half] = (pb[h, at, half].astype(F32) + rbh[h, half].astype(F32)).astype(BF16)
+            send(pb.at[h, at], rb.at[h, half], h, "rsb", d, x_peer(d))
 
     def second(h, d):
         at = mod4(x - d)
         arrived(ra.at[h, at], h, "rsa", d)
-        if d:
-            pa[h, at, zl] = (pa[h, at, zl].astype(F32) + ra[h, at].astype(F32)).astype(BF16)
-            send(pa.at[h, at, zl], ra2.at[h, x], h, "rsa2", 4 - d, dev(zh, y, c, zl, at))
+        if d == 2:
+            pz[h, 2] = (pf[h, at] + ra[h, at].astype(F32)).astype(BF16)
+            for half, e in ((0, 1), (1, 3)):
+                rows = pl.ds(half * (R // 2), R // 2)
+                send(pz.at[h, 2, rows], rah.at[h, half], h, "rsa2", 2 - 2 * half, x_peer(e))
+
+    def pass_a(h):
+        for half, d in ((0, 1), (1, 3)):
+            at = mod4(x + d)
+            arrived(rah.at[h, half], h, "rsa2", 2 - 2 * half)
+            for part in range(2):
+                rows = slice(part * (R // 2), (part + 1) * (R // 2))
+                v = pf[h, at, rows] + ra[h, at, rows].astype(F32)
+                if part == half:
+                    v = v + rah[h, half].astype(F32)
+                pz[h, half, rows] = v.astype(BF16)
+            send(pz.at[h, half], ra2.at[h, half], h, "rsa2", d, x_peer(d))
 
     def swiglu(v, w):
         g, u = v[:, 0:w], v[:, w:2 * w]
@@ -258,24 +284,21 @@
 
     def sum_b(h, t):
         v = pb[h, x, t].astype(F32)
-        for d in (1, 2, 3):
-            v = v + rb[h, mod4(x - d), t].astype(F32)
-        return v
+        return v + rb[h, 0, t].astype(F32) + rb[h, 1, t].astype(F32)
 
     def second_b(h):
-        for d in (1, 3, 2):
-            arrived(rb.at[h, mod4(x - d)], h, "rsb", d)
+        for half, d in ((0, 1), (1, 3)):
+            arrived(rb.at[h, half], h, "rsb", d)
         sbf[h] = sum_b(h, 1 - zl).astype(BF16)
         send(sbf.at[h], rb2.at[h], h, "rsb2", 0, partner)
 
     def hidden(h):
         arrived(rb2.at[h], h, "rsb2", 0)
         hb[h, zh, zl, :, WA:COLS] = swiglu(sum_b(h, zl) + rb2[h].astype(F32), WB)
-        for d in (1, 3, 2):
-            arrived(ra2.at[h, mod4(x - d)], h, "rsa2", d)
-        va = pa[h, x, zl].astype(F32) + ra[h, x].astype(F32)
-        for d in (1, 2, 3):
-            va = va + ra2[h, mod4(x - d)].astype(F32)
+        for half, d in ((0, 1), (1, 3)):
+            arrived(ra2.at[h, half], h, "rsa2", d)
+        va = pf[h, x] + ra[h, x].astype(F32)
+        va = va + ra2[h, 0].astype(F32) + ra2[h, 1].astype(F32)
         hb[h, zh, zl, :, 0:WA] = swiglu(va, WA)
 
     def gram(h, row, flipped, panel, total, w):
@@ -360,6 +383,8 @@
         "R2": lambda h: row_second(h, "X", raw, xf),
         "R3": lambda h: row_third(h, "X", xf),
         "S": second,
+        "PB": pass_b,
+        "SA": pass_a,
         "SB": second_b,
         "HID": step_hid,
         "HR1": lambda h: row_first(h, "H", hb, hf),
@@ -389,9 +414,9 @@
         vm(NH, 2, 2, R, FEAT), vm(NH, 8, 8, 2 * R, dtype=F32), vm(NH, 4, 8, 2 * R, dtype=F32),
         vm(NH, 4, 2, R, FEAT), vm(NH, 4, 2, R, FEAT), vm(NH, 2, 4, 2, R, FEAT),
         vm(DEPTH, COLS), vm(DEPTH, COLS),
-        vm(NH, 4, 2, R, 2 * WA), vm(NH, 4, 2, R, 2 * WB),
-        vm(NH, 4, R, 2 * WA), vm(NH, 4, R, 2 * WA),
-        vm(NH, 4, 2, R, 2 * WB), vm(NH, R, 2 * WB), vm(NH, R, 2 * WB),
+        vm(NH, 4, R, 2 * WA), vm(NH, 4, R, 2 * WA, dtype=F32), vm(NH, 3, R, 2 * WA), vm(NH, 4, 2, R, 2 * WB),
+        vm(NH, 4, R, 2 * WA), vm(NH, 2, R // 2, 2 * WA), vm(NH, 2, R, 2 * WA),
+        vm(NH, 2, 2, R, 2 * WB), vm(NH, 2, R, 2 * WB), vm(NH, R, 2 * WB), vm(NH, R, 2 * WB),
         vm(NH, 2, 2, R, COLS), vm(NH, 4, 2, R, COLS), vm(NH, 4, 2, R, COLS), vm(NH, 2, 4, 2, R, COLS),
         vm(FEAT, 8 * R), vm(COLS, 8 * R),
         vm(FEAT, 2 * FEAT, dtype=F32), vm(COLS, 2 * COLS, dtype=F32),
@@ -422,7 +447,7 @@
 
 
 def last_part(gin, ghid, left, right):
-    n = 8
+    n = 2
 
     def rows(a):
         return pl.BlockSpec((a.shape[0] // n, a.shape[1]), lambda i: (i, 0))

time: 162 us -> 154 us (0.951)
  Pallas kernels: 161 us -> 153 us
    pallas_call x1, Pallas kernels: 151 us -> 146 us  [grams(): pl.pallas_call(kernel, out_shape=[jax.ShapeDtypeStruct(shape, dtype) for...]
    pallas_call x1, Pallas kernels: 9.85 us -> 6.93 us  [last_part(): pl.pallas_call(last_kernel, grid=(n,), out_shape=[jax.ShapeDtypeStruct(a....]
where the time goes in v4:
time: 154 us; the launch traced here: 153 us
  Pallas kernels  153 us (99%)
    pallas_call x1, Pallas kernels, grams(): pl.pallas_call(kernel, out_shape=[jax.ShapeDtypeStruct(shape, dtype) for...  146 us
    pallas_call x1, Pallas kernels, last_part(): pl.pallas_call(last_kernel, grid=(n,), out_shape=[jax.ShapeDtypeStruct(a....  6.93 us

profile of v4, /device:TPU:1, one launch (start us, length us, event | category | flops | bytes accessed | tf_op | source)
XLA Modules:
  0.0 153.4 jit_solution(8263326483871071769)
XLA Ops:
  0.6 145.8 %shard_map.68 = (f32[512,1024]{1,0:T(8,128)}, f32[768,1536]{1,0:T(8,128)}, bf16[768,512]{1,0:T(8,128)(2,1)}, bf16[4,2,64,1536]{3,2,1,0:T(8,128)(2,1)}) custom-call(bf16[256,512]{1,0:T(8,128)(2,1)} %tok_ref.1, s32[2,128]{1,0:T(2,128)} %bitcast.5, f32[16,1,512]{2,1,0:T(1,128)} %bitcast.4, bf16[1024,768]{1,0:T(8,128)(2,1)} %wg_hbm.1, bf16[1024,768]{1,0:T(8,128)(2,1)} %wu_hbm.1), custom_call_target="tpu_custom_call" | custom-call | flops 12999999488 | bytes 10485760 | tf_op jit(solution)/shard_map/pallas_call | solution.py:430
  146.4 6.9 %shard_map.69 = (f32[512,1024]{1,0:T(8,128)}, f32[768,1536]{1,0:T(8,128)}) custom-call(f32[512,1024]{1,0:T(8,128)} %get-tuple-element.6.gin, f32[768,1536]{1,0:T(8,128)} %get-tuple-element.7.ghid, bf16[768,512]{1,0:T(8,128)(2,1)} %get-tuple-element.8.left, bf16[512,1536]{1,0:T(8,128)(2,1)} %bitcast.3), custom_call_target="tpu_custom_call" | custom-call | flops 1207959552 | bytes 16777216 | tf_op jit(solution)/shard_map/pallas_call | solution.py:455
